TPU v7x, 32 devices: a whole 2x2x4 slice. The times are simulated.
32 devices in a mesh: sector: 16 (over z, y, core), lift: 2 (over x).
Axes of the slice: x: 2, y: 2, z: 4, core: 2. Of those that a mesh axis runs over, the one named last changes fastest.
Arguments:
- right_side: float32 [128, 65536], P('lift', 'sector'), may hold values from -40 to 40
- diagonal: float32 [65536], P('sector'), may hold values from 1.9 to 2.6
- coupling: float32 [65536], P('sector'), may hold values from 0.3 to 0.94
- local_inverse: bfloat16 [64, 1024, 2048], P('sector'), may hold values from -0.1 to 0.6
- coarse_basis: bfloat16 [64, 16, 1024], P('sector'), may hold values from -0.1875 to 0.1875
- coarse_inverse: float32 [1024, 1024], P('sector', 'lift'), may hold values from -8 to 12
Outputs:
- solution: float32 [128, 65536], P('lift', 'sector')
- residual: float32 [128, 65536], P('lift', 'sector')
All inputs are finite; a program needn't handle non-finite values.
Results may differ from a plain program's by a relative error of at most 0.019.
Values may be sent and summed in bfloat16 or wider, within the bound.
A program may use at most 128 MiB of HBM per device.

v0:
```python
import functools

import jax
import jax.numpy as jnp
from jax import lax
from jax.experimental import pallas as pl
from jax.experimental.pallas import tpu as pltpu
from jax.sharding import PartitionSpec as P

SWEEPS = 4
OUTER = 2
LANE = 128
F32 = jnp.float32
BF16 = jnp.bfloat16
NT = (((1,), (1,)), ((), ()))


def dot_nt(a, b):
    return lax.dot_general(a, b, NT, preferred_element_type=F32)


def kernel(
    ns, nl,
    rhs_ref, diag_ref, coup_ref, inv_ref, basis_ref, cinv_ref,
    sol_ref, res_ref,
    wv, u, img, h, snd, rcv, edge, esnd, ercv, bext, cx, gbuf, stat, sbuf,
    w_sem, hs_sem, hr_sem, es_sem, er_sem, ls_sem, lr_sem, ns_sem, nr_sem,
    gs_sem, gr_sem, ss_sem, sr_sem,
):
    cases, rows = rhs_ref.shape
    subs, own, order = inv_ref.shape
    margin = (order - own) // 2
    modes = basis_ref.shape[1]
    nm = subs * modes
    tile = wv.shape[1] // w_sem.shape[0]
    tiles = own // tile
    group = 16
    groups = cases // group
    cut = margin + 2 * LANE
    me = lax.axis_index("sector")
    lift = lax.axis_index("lift")
    right = lax.rem(me + 1, ns)
    left = lax.rem(me + ns - 1, ns)

    def w_copy(i):
        return pltpu.make_async_copy(
            inv_ref.at[:, pl.ds(i * tile, tile), :], wv.at[:, pl.ds(i * tile, tile), :], w_sem.at[i]
        )

    for i in range(tiles):
        w_copy(i).start()

    def remote(src, dst, send, recv, where):
        return pltpu.make_async_remote_copy(
            src_ref=src, dst_ref=dst, send_sem=send, recv_sem=recv,
            device_id=where, device_id_type=pl.DeviceIdType.MESH,
        )

    bext[...] = jnp.zeros_like(bext)
    for j in range(subs):
        bext[j * modes:(j + 1) * modes, LANE + j * own:LANE + (j + 1) * own] = basis_ref[j]
    cx[...] = jnp.zeros_like(cx)
    half = cinv_ref.shape[1]
    per = half // nm
    lanes = lax.broadcasted_iota(jnp.int32, (nm, LANE), 1)
    for d in range(per):
        start = d * nm
        base = (start // LANE) * LANE
        block = cinv_ref[:, base:base + LANE]
        if start > base:
            block = pltpu.roll(block, LANE - (start - base), 1)
        block = jnp.where(lanes < nm, block, 0.0).astype(BF16)
        cx[0:nm, pl.ds(pl.multiple_of((lift * per + d) * LANE, LANE), LANE)] = block
    res_ref[...] = rhs_ref[...]
    sol_ref[...] = jnp.zeros_like(sol_ref)

    barrier = pltpu.get_barrier_semaphore()

    def greet(k, carry):
        pl.semaphore_signal(
            barrier, inc=1, device_id={"sector": lax.rem(me + k, ns)},
            device_id_type=pl.DeviceIdType.MESH,
        )
        return carry

    lax.fori_loop(1, ns, greet, 0)
    for k in range(1, nl):
        pl.semaphore_signal(
            barrier, inc=1, device_id={"lift": lax.rem(lift + k, nl)},
            device_id_type=pl.DeviceIdType.MESH,
        )
    pl.semaphore_wait(barrier, ns - 1 + nl - 1)

    def lift_copy(k):
        part = cx.at[0:nm, pl.ds(pl.multiple_of(lift * per * LANE, LANE), per * LANE)]
        return remote(part, part, ls_sem.at[k], lr_sem.at[k], {"lift": lax.rem(lift + k, nl)})

    def lift_wait(k):
        source = lax.rem(lift + nl - k, nl)
        part = cx.at[0:nm, pl.ds(pl.multiple_of(source * per * LANE, LANE), per * LANE)]
        return remote(part, part, ls_sem.at[k], lr_sem.at[k], {"lift": lax.rem(lift + k, nl)})

    def neighbour_copies():
        return (
            remote(cx.at[nm - modes:nm], cx.at[nm:nm + modes], ns_sem.at[0], nr_sem.at[0], {"sector": right}),
            remote(cx.at[0:modes], cx.at[nm + modes:nm + 2 * modes], ns_sem.at[1], nr_sem.at[1], {"sector": left}),
            remote(
                basis_ref.at[subs - 1, :, own - LANE:own], bext.at[nm:nm + modes, 0:LANE],
                ns_sem.at[2], nr_sem.at[2], {"sector": right},
            ),
            remote(
                basis_ref.at[0, :, 0:LANE], bext.at[nm + modes:nm + 2 * modes, LANE + rows:2 * LANE + rows],
                ns_sem.at[3], nr_sem.at[3], {"sector": left},
            ),
        )

    for k in range(1, nl):
        lift_copy(k).start()

    lane_g = lax.broadcasted_iota(jnp.int32, (group, LANE), 1)
    lane_c = lax.broadcasted_iota(jnp.int32, (cases, LANE), 1)
    eye = lax.broadcasted_iota(jnp.int32, (cases, LANE), 0) == lane_c

    def pack(parts):
        out = jnp.zeros((parts[0].shape[0], LANE), F32)
        lane = lane_g
        for at, part in enumerate(parts):
            high = part.astype(BF16).astype(F32)
            out = jnp.where(lane == 2 * at, high, out)
            out = jnp.where(lane == 2 * at + 1, part - high, out)
        return out.astype(BF16)

    def applied(rs, c):
        x = u[rs, c * own:c * own + own + 2 * LANE]
        width = own + 2 * LANE
        both = pltpu.roll(x, 1, 1)[:, LANE:LANE + own] + pltpu.roll(x, width - 1, 1)[:, LANE:LANE + own]
        cols = slice(c * own, (c + 1) * own)
        return diag_ref[:, cols] * x[:, LANE:LANE + own] - coup_ref[:, cols] * both

    def halo_copies(t):
        return (
            remote(snd.at[0], rcv.at[t, 0], hs_sem.at[t, 0], hr_sem.at[t, 0], {"sector": left}),
            remote(snd.at[1], rcv.at[t, 1], hs_sem.at[t, 1], hr_sem.at[t, 1], {"sector": right}),
        )

    def rim_copies(o):
        return (
            remote(esnd.at[0], ercv.at[o, 0], es_sem.at[o, 0], er_sem.at[o, 0], {"sector": left}),
            remote(esnd.at[1], ercv.at[o, 1], es_sem.at[o, 1], er_sem.at[o, 1], {"sector": right}),
        )

    def gather_copy(o, k):
        return remote(
            gbuf.at[o, :, pl.ds(pl.multiple_of(me * LANE, LANE), LANE)],
            gbuf.at[o, :, pl.ds(pl.multiple_of(me * LANE, LANE), LANE)],
            gs_sem.at[o, k], gr_sem.at[o, k], {"sector": lax.rem(me + k, ns)},
        )

    def gather_wait(o, k):
        source = lax.rem(me + ns - k, ns)
        part = gbuf.at[o, :, pl.ds(pl.multiple_of(source * LANE, LANE), LANE)]
        return remote(part, part, gs_sem.at[o, k], gr_sem.at[o, k], {"sector": lax.rem(me + k, ns)})

    def sum_copy(o, k):
        return remote(
            sbuf.at[o, me], sbuf.at[o, me], ss_sem.at[o, k], sr_sem.at[o, k],
            {"sector": lax.rem(me + k, ns)},
        )

    def sum_wait(o, k):
        source = lax.rem(me + ns - k, ns)
        return remote(
            sbuf.at[o, source], sbuf.at[o, source], ss_sem.at[o, k], sr_sem.at[o, k],
            {"sector": lax.rem(me + k, ns)},
        )

    def sweep(t, carry):
        def residual_rows(g, carry):
            rs = pl.ds(pl.multiple_of(g * group, group), group)
            for c in range(subs):
                hf = res_ref[rs, c * own:(c + 1) * own] - applied(rs, c)
                hb = hf.astype(BF16)
                h[rs, c * own:(c + 1) * own] = hb
                if c == 0:
                    snd[0, rs, 0:margin] = hb[:, 0:margin]
                    edge[0, rs, :] = hf[:, 0:LANE]
                    snd[0, rs, margin:margin + LANE] = pack(
                        [u[rs, LANE:LANE + 1], hf[:, 0:1], jnp.broadcast_to(coup_ref[:, 0:1], (group, 1))]
                    )
                if c == subs - 1:
                    snd[1, rs, 0:margin] = hb[:, own - margin:own]
                    edge[1, rs, :] = hf[:, own - LANE:own]
                    snd[1, rs, margin:margin + LANE] = pack(
                        [
                            u[rs, LANE + rows - 1:LANE + rows], hf[:, own - 1:own],
                            jnp.broadcast_to(coup_ref[:, rows - 1:rows], (group, 1)),
                        ]
                    )
            return carry

        lax.fori_loop(0, groups, residual_rows, 0)
        to_left, to_right = halo_copies(t)
        to_left.start()
        to_right.start()

        def inner(i, carry):
            @pl.when(t == 0)
            def _():
                w_copy(i).wait()

            ws = pl.ds(pl.multiple_of(i * tile, tile), tile)
            for j in range(subs):
                low = cut if j == 0 else 0
                high = order - cut if j == subs - 1 else order
                shift = j * own - margin
                out = pl.ds(pl.multiple_of(LANE + j * own + i * tile, LANE), tile)
                u[:, out] += dot_nt(h[:, shift + low:shift + high], wv[j, ws, low:high])
            return carry

        lax.fori_loop(0, tiles, inner, 0, unroll=False)
        to_left.wait()
        to_right.wait()
        msg_high = rcv[t, 0, :, margin:margin + LANE].astype(F32)
        msg_low = rcv[t, 1, :, margin:margin + LANE].astype(F32)
        mine_low = snd[0, :, margin:margin + LANE].astype(F32)
        mine_high = snd[1, :, margin:margin + LANE].astype(F32)

        def part(msg, at):
            return msg[:, 2 * at:2 * at + 1] + msg[:, 2 * at + 1:2 * at + 2]

        tile_low = edge[0]
        h[:, 0:LANE] = jnp.where(
            lane_c == 0, tile_low + coup_ref[:, 0:LANE] * part(msg_low, 0), tile_low
        ).astype(BF16)
        tile_high = edge[1]
        h[:, rows - LANE:rows] = jnp.where(
            lane_c == LANE - 1, tile_high + coup_ref[:, rows - LANE:rows] * part(msg_high, 0), tile_high
        ).astype(BF16)
        halo_low = rcv[t, 1, :, margin - LANE:margin].astype(F32)
        rcv[t, 1, :, margin - LANE:margin] = jnp.where(
            lane_c == LANE - 1, part(msg_low, 1) + part(msg_low, 2) * part(mine_low, 0), halo_low
        ).astype(BF16)
        halo_high = rcv[t, 0, :, 0:LANE].astype(F32)
        rcv[t, 0, :, 0:LANE] = jnp.where(
            lane_c == 0, part(msg_high, 1) + part(msg_high, 2) * part(mine_high, 0), halo_high
        ).astype(BF16)

        def outer_part(i, carry):
            ws = pl.ds(pl.multiple_of(i * tile, tile), tile)
            out = pl.ds(pl.multiple_of(LANE + i * tile, LANE), tile)
            u[:, out] += dot_nt(rcv[t, 1, :, 0:margin], wv[0, ws, 0:margin]) + dot_nt(
                h[:, 0:cut - margin], wv[0, ws, margin:cut]
            )
            out = pl.ds(pl.multiple_of(LANE + (subs - 1) * own + i * tile, LANE), tile)
            u[:, out] += dot_nt(rcv[t, 0, :, 0:margin], wv[subs - 1, ws, order - margin:order]) + dot_nt(
                h[:, rows - (cut - margin):rows], wv[subs - 1, ws, order - cut:order - margin]
            )
            return carry

        lax.fori_loop(0, tiles, outer_part, 0, unroll=False)
        return carry

    def correction(o, carry):
        u[...] = jnp.zeros_like(u)
        lax.fori_loop(o * SWEEPS, (o + 1) * SWEEPS, sweep, 0, unroll=False)

        @pl.when(o == 0)
        def _():
            for k in range(1, nl):
                lift_wait(k).wait()
            for copy in neighbour_copies():
                copy.start()

        for g in range(groups):
            rs = slice(g * group, (g + 1) * group)
            esnd[0, rs, :] = pack([u[rs, LANE:LANE + 1]])
            esnd[1, rs, :] = pack([u[rs, LANE + rows - 1:LANE + rows]])
        to_left, to_right = rim_copies(o)
        to_left.start()
        to_right.start()
        to_left.wait()
        to_right.wait()
        msg = ercv[o, 1].astype(F32)
        u[:, 0:LANE] = jnp.broadcast_to(msg[:, 0:1] + msg[:, 1:2], (cases, LANE))
        msg = ercv[o, 0].astype(F32)
        u[:, LANE + rows:2 * LANE + rows] = jnp.broadcast_to(msg[:, 0:1] + msg[:, 1:2], (cases, LANE))

        def coarse_rows(g, carry):
            rs = pl.ds(pl.multiple_of(g * group, group), group)
            for c in range(subs):
                cols = slice(c * own, (c + 1) * own)
                h[rs, cols] = (res_ref[rs, cols] - applied(rs, c)).astype(BF16)
            return carry

        lax.fori_loop(0, groups, coarse_rows, 0)
        projected = dot_nt(h[...], bext[:, LANE:LANE + rows])
        gbuf[o, :, pl.ds(pl.multiple_of(me * LANE, LANE), LANE)] = projected.astype(BF16)

        def start_gather(k, carry):
            gather_copy(o, k).start()
            return carry

        lax.fori_loop(1, ns, start_gather, 0)

        def wait_gather(k, carry):
            gather_wait(o, k).wait()
            return carry

        lax.fori_loop(1, ns, wait_gather, 0)

        @pl.when(o == 0)
        def _():
            for copy in neighbour_copies():
                copy.wait()

        coarse = dot_nt(gbuf[o], cx[...]).astype(BF16)
        width = 2 * LANE + rows
        step = 2 * LANE
        for at in range(0, width, step):
            u[:, at:at + step] += jnp.dot(coarse, bext[:, at:at + step], preferred_element_type=F32)

        def image_rows(g, carry):
            rs = pl.ds(pl.multiple_of(g * group, group), group)
            first = jnp.zeros((group, LANE), F32)
            second = jnp.zeros((group, LANE), F32)
            for c in range(subs):
                cols = slice(c * own, (c + 1) * own)
                value = applied(rs, c)
                img[rs, cols] = value
                cross = res_ref[rs, cols] * value
                square = value * value
                for at in range(0, own, LANE):
                    first += cross[:, at:at + LANE]
                    second += square[:, at:at + LANE]
            stat[0, rs, :] = first
            stat[1, rs, :] = second
            return carry

        lax.fori_loop(0, groups, image_rows, 0)
        line = lax.broadcasted_iota(jnp.int32, (8, LANE), 0)
        row_sums = [
            jnp.sum(jnp.where(eye, jnp.sum(stat[at], axis=1, keepdims=True), 0.0), axis=0, keepdims=True)
            for at in range(2)
        ]
        sbuf[o, me] = jnp.where(line == 0, row_sums[0], jnp.where(line == 1, row_sums[1], 0.0))

        def start_sum(k, carry):
            sum_copy(o, k).start()
            return carry

        lax.fori_loop(1, ns, start_sum, 0)

        def wait_sum(k, carry):
            sum_wait(o, k).wait()
            return carry

        lax.fori_loop(1, ns, wait_sum, 0)
        totals = jnp.sum(sbuf[o], axis=0)
        alpha_row = totals[0:1] / (totals[1:2] + 1e-06)
        stat[0] = jnp.broadcast_to(
            jnp.sum(jnp.where(eye, alpha_row, 0.0), axis=1, keepdims=True), (cases, LANE)
        )

        def step_rows(g, carry):
            rs = pl.ds(pl.multiple_of(g * group, group), group)
            alpha = stat[0, rs, 0:1]
            for c in range(subs):
                cols = slice(c * own, (c + 1) * own)
                sol_ref[rs, cols] += alpha * u[rs, LANE + c * own:LANE + (c + 1) * own]
                res_ref[rs, cols] -= alpha * img[rs, cols]
            return carry

        lax.fori_loop(0, groups, step_rows, 0)
        return carry

    lax.fori_loop(0, OUTER, correction, 0, unroll=False)


def body(right_side, diagonal, coupling, local_inverse, coarse_basis, coarse_inverse):
    ns = lax.axis_size("sector")
    nl = lax.axis_size("lift")
    cases, rows = right_side.shape
    subs, own, order = local_inverse.shape
    modes = coarse_basis.shape[1]
    margin = (order - own) // 2
    steps = SWEEPS * OUTER
    tile = 256
    vmem = pl.BlockSpec(memory_space=pltpu.VMEM)
    dma = pltpu.SemaphoreType.DMA
    flops = 2 * cases * subs * own * order * steps
    return pl.pallas_call(
        functools.partial(kernel, ns, nl),
        out_shape=(
            jax.ShapeDtypeStruct((cases, rows), F32),
            jax.ShapeDtypeStruct((cases, rows), F32),
        ),
        in_specs=[vmem, vmem, vmem, pl.BlockSpec(memory_space=pl.ANY), vmem, vmem],
        out_specs=(vmem, vmem),
        scratch_shapes=[
            pltpu.VMEM((subs, own, order), BF16),
            pltpu.VMEM((cases, rows + 2 * LANE), F32),
            pltpu.VMEM((cases, rows), F32),
            pltpu.VMEM((cases, rows), BF16),
            pltpu.VMEM((2, cases, margin + LANE), BF16),
            pltpu.VMEM((steps, 2, cases, margin + LANE), BF16),
            pltpu.VMEM((2, cases, LANE), F32),
            pltpu.VMEM((2, cases, LANE), BF16),
            pltpu.VMEM((OUTER, 2, cases, LANE), BF16),
            pltpu.VMEM((LANE, rows + 2 * LANE), BF16),
            pltpu.VMEM((LANE, ns * LANE), BF16),
            pltpu.VMEM((OUTER, cases, ns * LANE), BF16),
            pltpu.VMEM((2, cases, LANE), F32),
            pltpu.VMEM((OUTER, ns, 8, LANE), F32),
            dma((own // tile,)),
            dma((steps, 2)), dma((steps, 2)),
            dma((OUTER, 2)), dma((OUTER, 2)),
            dma((nl,)), dma((nl,)),
            dma((4,)), dma((4,)),
            dma((OUTER, ns)), dma((OUTER, ns)),
            dma((OUTER, ns)), dma((OUTER, ns)),
        ],
        compiler_params=pltpu.CompilerParams(
            collective_id=0, has_side_effects=True, vmem_limit_bytes=56 * 1024 * 1024
        ),
        cost_estimate=pl.CostEstimate(
            flops=flops, bytes_accessed=2 * subs * own * order, transcendentals=0
        ),
    )(right_side, diagonal[None, :], coupling[None, :], local_inverse, coarse_basis, coarse_inverse)


def solution(mesh):
    in_specs = (
        P("lift", "sector"),
        P("sector"),
        P("sector"),
        P("sector", None, None),
        P("sector", None, None),
        P("sector", "lift"),
    )
    out_specs = (P("lift", "sector"), P("lift", "sector"))
    return jax.shard_map(body, mesh=mesh, in_specs=in_specs, out_specs=out_specs, check_vma=False)
```

profile of v0, /device:TPU:0, one launch (start us, length us, event | category | flops | bytes accessed | tf_op | source)
XLA Modules:
  0.0 115.1 jit_solution(10962285712513259808)
XLA Ops:
  0.6 109.9 %shard_map.77 = (f32[64,4096]{1,0:T(8,128)}, f32[64,4096]{1,0:T(8,128)}) custom-call(f32[64,4096]{1,0:T(8,128)} %rhs_ref.1, f32[1,4096]{1,0:T(1,128)} %bitcast.2, f32[1,4096]{1,0:T(1,128)} %bitcast.3, bf16[4,1024,2048]{2,1,0:T(8,128)(2,1)} %inv_ref.1, bf16[4,16,1024]{2,1,0:T(8,128)(2,1)} %basis_ref.1, f32[64,512]{1,0:T(8,128)} %cinv_ref.1), custom_call_target="tpu_custom_call" | custom-call | flops 8589934592 | bytes 16777216 | tf_op jit(solution)/shard_map/pallas_call | solution.py:391
  110.5 2.3 %copy.10 = f32[64,4096]{1,0:T(8,128)} copy(f32[64,4096]{1,0:T(8,128)} %get-tuple-element.4) | data formatting | bytes 2097152
  112.8 2.3 %copy.11 = f32[64,4096]{1,0:T(8,128)} copy(f32[64,4096]{1,0:T(8,128)} %get-tuple-element.5) | data formatting | bytes 2097152
where the time goes:
time: 115 us
  Pallas kernels  110 us (96%)
  local copies, waits for them, and re-layouts  4.54 us (4%)
    pallas_call x1, Pallas kernels, body(): pl.pallas_call(functools.partial(kernel, ns, nl), out_shape=(jax.ShapeDty...  110 us
    unnamed x2, local copies, waits for them, and re-layouts  4.54 us

commit v1 on v0

--- a/solution.py
+++ b/solution.py
@@ -19,11 +19,15 @@
     return lax.dot_general(a, b, NT, preferred_element_type=F32)
 
 
+def times(field, inverse):
+    return dot_nt(inverse, field)
+
+
 def kernel(
     ns, nl,
     rhs_ref, diag_ref, coup_ref, inv_ref, basis_ref, cinv_ref,
-    sol_ref, res_ref,
-    wv, u, img, h, snd, rcv, edge, esnd, ercv, bext, cx, gbuf, stat, sbuf,
+    sol_ref, res_ref, last_ref, img, alpha_ref,
+    wv, u, h, snd, rcv, edge, esnd, ercv, bext, cx, gbuf, stat, sbuf,
     w_sem, hs_sem, hr_sem, es_sem, er_sem, ls_sem, lr_sem, ns_sem, nr_sem,
     gs_sem, gr_sem, ss_sem, sr_sem,
 ):
@@ -214,7 +218,7 @@
                 high = order - cut if j == subs - 1 else order
                 shift = j * own - margin
                 out = pl.ds(pl.multiple_of(LANE + j * own + i * tile, LANE), tile)
-                u[:, out] += dot_nt(h[:, shift + low:shift + high], wv[j, ws, low:high])
+                u[:, out] += times(h[:, shift + low:shift + high], wv[j, ws, low:high]).T
             return carry
 
         lax.fori_loop(0, tiles, inner, 0, unroll=False)
@@ -248,13 +252,15 @@
         def outer_part(i, carry):
             ws = pl.ds(pl.multiple_of(i * tile, tile), tile)
             out = pl.ds(pl.multiple_of(LANE + i * tile, LANE), tile)
-            u[:, out] += dot_nt(rcv[t, 1, :, 0:margin], wv[0, ws, 0:margin]) + dot_nt(
-                h[:, 0:cut - margin], wv[0, ws, margin:cut]
-            )
+            u[:, out] += (
+                times(rcv[t, 1, :, 0:margin], wv[0, ws, 0:margin])
+                + times(h[:, 0:cut - margin], wv[0, ws, margin:cut])
+            ).T
             out = pl.ds(pl.multiple_of(LANE + (subs - 1) * own + i * tile, LANE), tile)
-            u[:, out] += dot_nt(rcv[t, 0, :, 0:margin], wv[subs - 1, ws, order - margin:order]) + dot_nt(
-                h[:, rows - (cut - margin):rows], wv[subs - 1, ws, order - cut:order - margin]
-            )
+            u[:, out] += (
+                times(rcv[t, 0, :, 0:margin], wv[subs - 1, ws, order - margin:order])
+                + times(h[:, rows - (cut - margin):rows], wv[subs - 1, ws, order - cut:order - margin])
+            ).T
             return carry
 
         lax.fori_loop(0, tiles, outer_part, 0, unroll=False)
@@ -357,23 +363,27 @@
         lax.fori_loop(1, ns, wait_sum, 0)
         totals = jnp.sum(sbuf[o], axis=0)
         alpha_row = totals[0:1] / (totals[1:2] + 1e-06)
-        stat[0] = jnp.broadcast_to(
+        alpha_ref[...] = jnp.broadcast_to(
             jnp.sum(jnp.where(eye, alpha_row, 0.0), axis=1, keepdims=True), (cases, LANE)
         )
 
         def step_rows(g, carry):
             rs = pl.ds(pl.multiple_of(g * group, group), group)
-            alpha = stat[0, rs, 0:1]
+            alpha = alpha_ref[rs, 0:1]
             for c in range(subs):
                 cols = slice(c * own, (c + 1) * own)
                 sol_ref[rs, cols] += alpha * u[rs, LANE + c * own:LANE + (c + 1) * own]
                 res_ref[rs, cols] -= alpha * img[rs, cols]
             return carry
 
-        lax.fori_loop(0, groups, step_rows, 0)
+        @pl.when(o < OUTER - 1)
+        def _():
+            lax.fori_loop(0, groups, step_rows, 0)
+
         return carry
 
     lax.fori_loop(0, OUTER, correction, 0, unroll=False)
+    last_ref[...] = u[:, LANE:LANE + rows]
 
 
 def body(right_side, diagonal, coupling, local_inverse, coarse_basis, coarse_inverse):
@@ -388,18 +398,15 @@
     vmem = pl.BlockSpec(memory_space=pltpu.VMEM)
     dma = pltpu.SemaphoreType.DMA
     flops = 2 * cases * subs * own * order * steps
-    return pl.pallas_call(
+    solved, residual, update, image, alpha = pl.pallas_call(
         functools.partial(kernel, ns, nl),
-        out_shape=(
-            jax.ShapeDtypeStruct((cases, rows), F32),
-            jax.ShapeDtypeStruct((cases, rows), F32),
-        ),
+        out_shape=(jax.ShapeDtypeStruct((cases, rows), F32),) * 4
+        + (jax.ShapeDtypeStruct((cases, LANE), F32),),
         in_specs=[vmem, vmem, vmem, pl.BlockSpec(memory_space=pl.ANY), vmem, vmem],
-        out_specs=(vmem, vmem),
+        out_specs=(vmem,) * 5,
         scratch_shapes=[
             pltpu.VMEM((subs, own, order), BF16),
             pltpu.VMEM((cases, rows + 2 * LANE), F32),
-            pltpu.VMEM((cases, rows), F32),
             pltpu.VMEM((cases, rows), BF16),
             pltpu.VMEM((2, cases, margin + LANE), BF16),
             pltpu.VMEM((steps, 2, cases, margin + LANE), BF16),
@@ -426,6 +433,8 @@
             flops=flops, bytes_accessed=2 * subs * own * order, transcendentals=0
         ),
     )(right_side, diagonal[None, :], coupling[None, :], local_inverse, coarse_basis, coarse_inverse)
+    alpha = alpha[:, 0:1]
+    return solved + alpha * update, residual - alpha * image
 
 
 def solution(mesh):

time: 115 us -> 116 us (level)
  other arithmetic: 0 us -> 3.82 us
  local copies, waits for them, and re-layouts: 4.54 us -> 0.86 us
    unnamed x2 -> x0, local copies, waits for them, and re-layouts: 4.54 us -> none
    sub x0 -> x1, other arithmetic: none -> 3.82 us  [body(): return (solved + alpha * update, residual - alpha * image)]
where the time goes in v1:
time: 116 us
  Pallas kernels  111 us (96%)
  other arithmetic  3.82 us (3%)
    pallas_call x1, Pallas kernels, body(): pl.pallas_call(functools.partial(kernel, ns, nl), out_shape=(jax.ShapeDty...  111 us
    sub x1, other arithmetic, body(): return (solved + alpha * update, residual - alpha * image)  3.82 us

profile of v1, /device:TPU:0, one launch (start us, length us, event | category | flops | bytes accessed | tf_op | source)
XLA Modules:
  0.0 115.9 jit_solution(9853331076267475603)
XLA Ops:
  0.6 110.5 %shard_map.77 = (f32[64,4096]{1,0:T(8,128)}, f32[64,4096]{1,0:T(8,128)}, f32[64,4096]{1,0:T(8,128)}, f32[64,4096]{1,0:T(8,128)}, f32[64,128]{1,0:T(8,128)}) custom-call(f32[64,4096]{1,0:T(8,128)} %rhs_ref.1, f32[1,4096]{1,0:T(1,128)} %bitcast.2, f32[1,4096]{1,0:T(1,128)} %bitcast.3, bf16[4,1024,2048]{2,1,0:T(8,128)(2,1)} %inv_ref.1, ...), custom_call_target="tpu_custom_call" | custom-call | flops 8589934592 | bytes 16777216 | tf_op jit(solution)/shard_map/pallas_call | solution.py:401
  111.2 0.9 slice_reduce_fusion
  112.0 3.8 %multiply_subtract_fusion = (f32[64,4096]{1,0:T(8,128)}, f32[64,4096]{1,0:T(8,128)}) fusion(f32[64,4096]{1,0:T(8,128)} %get-tuple-element.10, f32[64,4096]{1,0:T(8,128)} %get-tuple-element.11, f32[64]{0:T(128)S(1)} %slice_reduce_fusion, f32[64,4096]{1,0:T(8,128)} %get-tuple-element.7, f32[64,4096]{1,0:T(8,128)} %get-tuple-element.9), kind=kLoop, calls=%fused_computation | loop fusion | flops 1048576 | bytes 6291712 | tf_op jit(solution)/shard_map/sub | solution.py:437

commit v2 on v1

v2 whole, which is shorter than its diff:
```python
import functools

import jax
import jax.numpy as jnp
from jax import lax
from jax.experimental import pallas as pl
from jax.experimental.pallas import tpu as pltpu
from jax.sharding import PartitionSpec as P

SWEEPS = 4
OUTER = 2
LANE = 128
F32 = jnp.float32
BF16 = jnp.bfloat16
NT = (((1,), (1,)), ((), ()))


def dot_nt(a, b):
    return lax.dot_general(a, b, NT, preferred_element_type=F32)


def times(field, inverse):
    return dot_nt(inverse, field)


def kernel(
    ns, nl,
    rhs_ref, diag_ref, coup_ref, inv_ref, basis_ref, cinv_ref,
    sol_out, res_out, last_out, img_out, alpha_ref,
    wv, u, keep, first, sol, field, h, snd, rcv, edge, esnd, ercv, bext, cx, cy, gbuf, stat, sbuf,
    r_sem, o_sem, w_sem, hs_sem, hr_sem, es_sem, er_sem, ls_sem, lr_sem, ns_sem, nr_sem,
    gs_sem, gr_sem, ss_sem, sr_sem,
):
    cases, rows = rhs_ref.shape
    subs, own, order = inv_ref.shape
    margin = (order - own) // 2
    modes = basis_ref.shape[1]
    nm = subs * modes
    tile = wv.shape[1] // w_sem.shape[0]
    tiles = own // tile
    group = 16
    groups = cases // group
    cut = margin + 2 * LANE
    me = lax.axis_index("sector")
    lift = lax.axis_index("lift")
    right = lax.rem(me + 1, ns)
    left = lax.rem(me + ns - 1, ns)

    def w_copy(i):
        return pltpu.make_async_copy(
            inv_ref.at[:, pl.ds(i * tile, tile), :], wv.at[:, pl.ds(i * tile, tile), :], w_sem.at[i]
        )

    rhs_copy = pltpu.make_async_copy(rhs_ref, field.at[0], r_sem)
    rhs_copy.start()
    for i in range(tiles):
        w_copy(i).start()
    result_copies = (
        pltpu.make_async_copy(sol, sol_out, o_sem.at[0]),
        pltpu.make_async_copy(field.at[0], res_out, o_sem.at[1]),
        pltpu.make_async_copy(u.at[:, LANE:LANE + rows], last_out, o_sem.at[2]),
        pltpu.make_async_copy(field.at[1], img_out, o_sem.at[3]),
    )

    def remote(src, dst, send, recv, where):
        return pltpu.make_async_remote_copy(
            src_ref=src, dst_ref=dst, send_sem=send, recv_sem=recv,
            device_id=where, device_id_type=pl.DeviceIdType.MESH,
        )

    bext[...] = jnp.zeros_like(bext)
    for j in range(subs):
        bext[j * modes:(j + 1) * modes, LANE + j * own:LANE + (j + 1) * own] = basis_ref[j]
    cx[...] = jnp.zeros_like(cx)
    half = cinv_ref.shape[1]
    per = half // nm
    lanes = lax.broadcasted_iota(jnp.int32, (nm, LANE), 1)
    for d in range(per):
        start = d * nm
        base = (start // LANE) * LANE
        block = cinv_ref[:, base:base + LANE]
        if start > base:
            block = pltpu.roll(block, LANE - (start - base), 1)
        block = jnp.where(lanes < nm, block, 0.0).astype(BF16)
        cx[0:nm, pl.ds(pl.multiple_of((lift * per + d) * LANE, LANE), LANE)] = block
    barrier = pltpu.get_barrier_semaphore()

    def greet(k, carry):
        pl.semaphore_signal(
            barrier, inc=1, device_id={"sector": lax.rem(me + k, ns)},
            device_id_type=pl.DeviceIdType.MESH,
        )
        return carry

    lax.fori_loop(1, ns, greet, 0)
    for k in range(1, nl):
        pl.semaphore_signal(
            barrier, inc=1, device_id={"lift": lax.rem(lift + k, nl)},
            device_id_type=pl.DeviceIdType.MESH,
        )
    h[...] = jnp.zeros_like(h)
    u[...] = jnp.zeros_like(u)
    sol[...] = jnp.zeros_like(sol)
    pl.semaphore_wait(barrier, ns - 1 + nl - 1)

    def lift_copy(k):
        part = cx.at[0:nm, pl.ds(pl.multiple_of(lift * per * LANE, LANE), per * LANE)]
        return remote(part, part, ls_sem.at[k], lr_sem.at[k], {"lift": lax.rem(lift + k, nl)})

    def lift_wait(k):
        source = lax.rem(lift + nl - k, nl)
        part = cx.at[0:nm, pl.ds(pl.multiple_of(source * per * LANE, LANE), per * LANE)]
        return remote(part, part, ls_sem.at[k], lr_sem.at[k], {"lift": lax.rem(lift + k, nl)})

    def neighbour_copies():
        return (
            remote(cx.at[nm - modes:nm], cx.at[nm:nm + modes], ns_sem.at[0], nr_sem.at[0], {"sector": right}),
            remote(cx.at[0:modes], cx.at[nm + modes:nm + 2 * modes], ns_sem.at[1], nr_sem.at[1], {"sector": left}),
            remote(
                basis_ref.at[subs - 1, :, own - LANE:own], bext.at[nm:nm + modes, 0:LANE],
                ns_sem.at[2], nr_sem.at[2], {"sector": right},
            ),
            remote(
                basis_ref.at[0, :, 0:LANE], bext.at[nm + modes:nm + 2 * modes, LANE + rows:2 * LANE + rows],
                ns_sem.at[3], nr_sem.at[3], {"sector": left},
            ),
        )

    for k in range(1, nl):
        lift_copy(k).start()

    lane_g = lax.broadcasted_iota(jnp.int32, (group, LANE), 1)
    lane_c = lax.broadcasted_iota(jnp.int32, (cases, LANE), 1)
    eye = lax.broadcasted_iota(jnp.int32, (cases, LANE), 0) == lane_c

    def pack(parts):
        out = jnp.zeros((parts[0].shape[0], LANE), F32)
        lane = lane_g
        for at, part in enumerate(parts):
            high = part.astype(BF16).astype(F32)
            out = jnp.where(lane == 2 * at, high, out)
            out = jnp.where(lane == 2 * at + 1, part - high, out)
        return out.astype(BF16)

    def applied(rs, at, width):
        x = u[rs, at:at + width + 2 * LANE]
        span = width + 2 * LANE
        both = pltpu.roll(x, 1, 1)[:, LANE:LANE + width] + pltpu.roll(x, span - 1, 1)[:, LANE:LANE + width]
        cols = slice(at, at + width)
        return diag_ref[:, cols] * x[:, LANE:LANE + width] - coup_ref[:, cols] * both

    def part(msg, at):
        return msg[:, 2 * at:2 * at + 1] + msg[:, 2 * at + 1:2 * at + 2]

    def halo_copies(t):
        return (
            remote(snd.at[0], rcv.at[t, 0], hs_sem.at[t, 0], hr_sem.at[t, 0], {"sector": right}),
            remote(snd.at[1], rcv.at[t, 1], hs_sem.at[t, 1], hr_sem.at[t, 1], {"sector": left}),
        )

    def rim_copies(o):
        return (
            remote(esnd.at[0], ercv.at[o, 0], es_sem.at[o, 0], er_sem.at[o, 0], {"sector": right}),
            remote(esnd.at[1], ercv.at[o, 1], es_sem.at[o, 1], er_sem.at[o, 1], {"sector": left}),
        )

    def gather_copy(o, k):
        return remote(
            gbuf.at[o, :, pl.ds(pl.multiple_of(me * LANE, LANE), LANE)],
            gbuf.at[o, :, pl.ds(pl.multiple_of(me * LANE, LANE), LANE)],
            gs_sem.at[o, k], gr_sem.at[o, k], {"sector": lax.rem(me + k, ns)},
        )

    def gather_wait(o, k):
        source = lax.rem(me + ns - k, ns)
        part = gbuf.at[o, :, pl.ds(pl.multiple_of(source * LANE, LANE), LANE)]
        return remote(part, part, gs_sem.at[o, k], gr_sem.at[o, k], {"sector": lax.rem(me + k, ns)})

    def sum_copy(o, k):
        return remote(
            sbuf.at[o, me], sbuf.at[o, me], ss_sem.at[o, k], sr_sem.at[o, k],
            {"sector": lax.rem(me + k, ns)},
        )

    def sum_wait(o, k):
        source = lax.rem(me + ns - k, ns)
        return remote(
            sbuf.at[o, source], sbuf.at[o, source], ss_sem.at[o, k], sr_sem.at[o, k],
            {"sector": lax.rem(me + k, ns)},
        )

    def sweep(t, src):
        def low_rows(g, carry):
            rs = pl.ds(pl.multiple_of(g * group, group), group)
            hf = field[src, rs, 0:margin] - applied(rs, 0, margin)
            hb = hf.astype(BF16)
            h[rs, LANE:LANE + margin] = hb
            snd[1, rs, 0:margin] = hb
            edge[0, rs, :] = hf[:, 0:LANE]
            snd[1, rs, margin:margin + LANE] = pack(
                [u[rs, LANE:LANE + 1], hf[:, 0:1], jnp.broadcast_to(coup_ref[:, 0:1], (group, 1))]
            )
            hf = field[src, rs, rows - margin:rows] - applied(rs, rows - margin, margin)
            hb = hf.astype(BF16)
            h[rs, LANE + rows - margin:LANE + rows] = hb
            snd[0, rs, 0:margin] = hb
            edge[1, rs, :] = hf[:, margin - LANE:margin]
            snd[0, rs, margin:margin + LANE] = pack(
                [
                    u[rs, LANE + rows - 1:LANE + rows], hf[:, margin - 1:margin],
                    jnp.broadcast_to(coup_ref[:, rows - 1:rows], (group, 1)),
                ]
            )
            return carry

        lax.fori_loop(0, groups, low_rows, 0, unroll=True)
        copies = halo_copies(t)
        for copy in copies:
            copy.start()

        def middle_rows(g, carry):
            rs = pl.ds(pl.multiple_of(g * group, group), group)
            for at in range(margin, rows - margin, own):
                width = min(own, rows - margin - at)
                hf = field[src, rs, at:at + width] - applied(rs, at, width)
                h[rs, LANE + at:LANE + at + width] = hf.astype(BF16)
            return carry

        lax.fori_loop(0, groups, middle_rows, 0)

        @pl.when(t == 0)
        def _():
            for k in range(1, nl):
                lift_wait(k).wait()
            for copy in neighbour_copies():
                copy.start()
            for i in range(tiles):
                w_copy(i).wait()

        def inner(i, carry):
            ws = pl.ds(pl.multiple_of(i * tile, tile), tile)
            for j in range(subs):
                low = cut if j == 0 else 0
                high = order - cut if j == subs - 1 else order
                shift = LANE + j * own - margin
                out = pl.ds(pl.multiple_of(LANE + j * own + i * tile, LANE), tile)
                u[:, out] += times(h[:, shift + low:shift + high], wv[j, ws, low:high]).T
            return carry

        lax.fori_loop(0, tiles, inner, 0, unroll=True)
        for copy in copies:
            copy.wait()
        msg_low = rcv[t, 0, :, margin:margin + LANE].astype(F32)
        msg_high = rcv[t, 1, :, margin:margin + LANE].astype(F32)
        mine_low = snd[1, :, margin:margin + LANE].astype(F32)
        mine_high = snd[0, :, margin:margin + LANE].astype(F32)
        tile_low = edge[0]
        h[:, LANE:2 * LANE] = jnp.where(
            lane_c == 0, tile_low + coup_ref[:, 0:LANE] * part(msg_low, 0), tile_low
        ).astype(BF16)
        tile_high = edge[1]
        h[:, rows:LANE + rows] = jnp.where(
            lane_c == LANE - 1, tile_high + coup_ref[:, rows - LANE:rows] * part(msg_high, 0), tile_high
        ).astype(BF16)
        halo_low = rcv[t, 0, :, margin - LANE:margin].astype(F32)
        rcv[t, 0, :, margin - LANE:margin] = jnp.where(
            lane_c == LANE - 1, part(msg_low, 1) + part(msg_low, 2) * part(mine_low, 0), halo_low
        ).astype(BF16)
        halo_high = rcv[t, 1, :, 0:LANE].astype(F32)
        rcv[t, 1, :, 0:LANE] = jnp.where(
            lane_c == 0, part(msg_high, 1) + part(msg_high, 2) * part(mine_high, 0), halo_high
        ).astype(BF16)

        def outer_part(i, carry):
            ws = pl.ds(pl.multiple_of(i * tile, tile), tile)
            out = pl.ds(pl.multiple_of(LANE + i * tile, LANE), tile)
            u[:, out] += (
                times(rcv[t, 0, :, 0:margin], wv[0, ws, 0:margin])
                + times(h[:, LANE:LANE + cut - margin], wv[0, ws, margin:cut])
            ).T
            out = pl.ds(pl.multiple_of(LANE + (subs - 1) * own + i * tile, LANE), tile)
            u[:, out] += (
                times(rcv[t, 1, :, 0:margin], wv[subs - 1, ws, order - margin:order])
                + times(
                    h[:, LANE + rows - (cut - margin):LANE + rows],
                    wv[subs - 1, ws, order - cut:order - margin],
                )
            ).T
            return carry

        lax.fori_loop(0, tiles, outer_part, 0, unroll=True)

    def complete_coarse():
        for copy in neighbour_copies():
            copy.wait()
        lane = lax.broadcasted_iota(jnp.int32, (LANE, LANE), 1)

        def fill(d, carry):
            def block(at):
                return cx[:, pl.ds(pl.multiple_of(at * LANE, LANE), LANE)].astype(F32)

            after = pltpu.roll(block(lax.rem(d + 1, ns)), nm + modes, 1)
            before = pltpu.roll(block(lax.rem(d + ns - 1, ns)), modes, 1)
            both = jnp.where(lane < nm + modes, before, after)
            both = jnp.where(lane < nm, block(d), jnp.where(lane < nm + 2 * modes, both, 0.0))
            cy[:, pl.ds(pl.multiple_of(d * LANE, LANE), LANE)] = both.astype(BF16)
            return carry

        lax.fori_loop(0, ns, fill, 0)

    def coarse_step(t, o):
        for g in range(groups):
            rs = slice(g * group, (g + 1) * group)
            esnd[0, rs, :] = pack([u[rs, LANE + rows - 1:LANE + rows]])
            esnd[1, rs, :] = pack([u[rs, LANE:LANE + 1]])
        rims = rim_copies(o)
        for copy in rims:
            copy.start()

        def coarse_rows(g, carry):
            rs = pl.ds(pl.multiple_of(g * group, group), group)
            for c in range(subs):
                cols = slice(c * own, (c + 1) * own)
                h[rs, LANE + c * own:LANE + (c + 1) * own] = (
                    field[0, rs, cols] - applied(rs, c * own, own)
                ).astype(BF16)
            return carry

        lax.fori_loop(0, groups, coarse_rows, 0)
        to_low = part(rcv[t, 0, :, margin:margin + LANE].astype(F32), 2) * u[:, LANE:LANE + 1]
        h[:, 0:LANE] = jnp.where(lane_c == LANE - 1, to_low, 0.0).astype(BF16)
        to_high = part(rcv[t, 1, :, margin:margin + LANE].astype(F32), 2) * u[:, LANE + rows - 1:LANE + rows]
        h[:, LANE + rows:2 * LANE + rows] = jnp.where(lane_c == 0, to_high, 0.0).astype(BF16)
        projected = dot_nt(h[...], bext[...])
        gbuf[o, :, pl.ds(pl.multiple_of(me * LANE, LANE), LANE)] = projected.astype(BF16)

        def start_gather(k, carry):
            gather_copy(o, k).start()
            return carry

        lax.fori_loop(1, ns, start_gather, 0)
        for copy in rims:
            copy.wait()
        msg = ercv[o, 0].astype(F32)
        u[:, 0:LANE] = jnp.broadcast_to(part(msg, 0), (cases, LANE))
        msg = ercv[o, 1].astype(F32)
        u[:, LANE + rows:2 * LANE + rows] = jnp.broadcast_to(part(msg, 0), (cases, LANE))

        def wait_gather(k, carry):
            gather_wait(o, k).wait()
            return carry

        lax.fori_loop(1, ns, wait_gather, 0)
        coarse = dot_nt(gbuf[o], cy[...]).astype(BF16)
        step = 2 * LANE
        for at in range(0, 2 * LANE + rows, step):
            u[:, at:at + step] += jnp.dot(coarse, bext[:, at:at + step], preferred_element_type=F32)

        def image_rows(g, carry):
            rs = pl.ds(pl.multiple_of(g * group, group), group)
            cross_sum = jnp.zeros((group, LANE), F32)
            square_sum = jnp.zeros((group, LANE), F32)
            for c in range(subs):
                cols = slice(c * own, (c + 1) * own)
                value = applied(rs, c * own, own)
                field[1, rs, cols] = value
                cross = field[0, rs, cols] * value
                square = value * value
                for at in range(0, own, LANE):
                    cross_sum += cross[:, at:at + LANE]
                    square_sum += square[:, at:at + LANE]
            stat[0, rs, :] = cross_sum
            stat[1, rs, :] = square_sum
            return carry

        lax.fori_loop(0, groups, image_rows, 0)
        line = lax.broadcasted_iota(jnp.int32, (8, LANE), 0)
        row_sums = [
            jnp.sum(jnp.where(eye, jnp.sum(stat[at], axis=1, keepdims=True), 0.0), axis=0, keepdims=True)
            for at in range(2)
        ]
        sbuf[o, me] = jnp.where(line == 0, row_sums[0], jnp.where(line == 1, row_sums[1], 0.0))

        def start_sum(k, carry):
            sum_copy(o, k).start()
            return carry

        lax.fori_loop(1, ns, start_sum, 0)

    def get_alpha(o):
        def wait_sum(k, carry):
            sum_wait(o, k).wait()
            return carry

        lax.fori_loop(1, ns, wait_sum, 0)
        totals = jnp.sum(sbuf[o], axis=0)
        alpha_row = totals[0:1] / (totals[1:2] + 1e-06)
        alpha_ref[...] = jnp.broadcast_to(
            jnp.sum(jnp.where(eye, alpha_row, 0.0), axis=1, keepdims=True), (cases, LANE)
        )

    def next_rows(g, carry):
        rs = pl.ds(pl.multiple_of(g * group, group), group)
        alpha = alpha_ref[rs, 0:1]
        for c in range(subs):
            cols = slice(c * own, (c + 1) * own)
            wide = slice(LANE + c * own, LANE + (c + 1) * own)
            sol[rs, cols] += alpha * keep[rs, cols]
            field[0, rs, cols] -= alpha * field[1, rs, cols]
            begun = first[rs, cols] - alpha * u[rs, wide]
            u[rs, wide] = begun
            if OUTER > 2:
                first[rs, cols] = begun
        return carry

    rhs_copy.wait()

    def turn(t, carry):
        o = t // SWEEPS
        begins = lax.rem(t, SWEEPS) == 0
        later = jnp.logical_and(begins, t > 0)
        sweep(t, jnp.where(later, 1, 0))

        @pl.when(t == 0)
        def _():
            first[...] = u[:, LANE:LANE + rows]
            complete_coarse()

        @pl.when(later)
        def _():
            get_alpha(o - 1)
            lax.fori_loop(0, groups, next_rows, 0)

        @pl.when(t == (OUTER - 1) * SWEEPS)
        def _():
            for copy in result_copies[:2]:
                copy.start()

        @pl.when(lax.rem(t, SWEEPS) == SWEEPS - 1)
        def _():
            coarse_step(t, o)

            @pl.when(o < OUTER - 1)
            def _():
                keep[...] = u[:, LANE:LANE + rows]
                u[...] = jnp.zeros_like(u)

        return carry

    lax.fori_loop(0, OUTER * SWEEPS, turn, 0, unroll=False)
    for copy in result_copies[2:]:
        copy.start()
    get_alpha(OUTER - 1)
    for copy in result_copies:
        copy.wait()


def last_kernel(alpha_ref, sol_ref, last_ref, res_ref, img_ref, sol_out, res_out):
    alpha = alpha_ref[:, 0:1]
    sol_out[...] = sol_ref[...] + alpha * last_ref[...]
    res_out[...] = res_ref[...] - alpha * img_ref[...]


def body(right_side, diagonal, coupling, local_inverse, coarse_basis, coarse_inverse):
    ns = lax.axis_size("sector")
    nl = lax.axis_size("lift")
    cases, rows = right_side.shape
    subs, own, order = local_inverse.shape
    modes = coarse_basis.shape[1]
    margin = (order - own) // 2
    steps = SWEEPS * OUTER
    tile = 256
    vmem = pl.BlockSpec(memory_space=pltpu.VMEM)
    hbm = pl.BlockSpec(memory_space=pl.ANY)
    dma = pltpu.SemaphoreType.DMA
    flops = 2 * cases * subs * own * order * steps
    solved, residual, update, image, alpha = pl.pallas_call(
        functools.partial(kernel, ns, nl),
        out_shape=(jax.ShapeDtypeStruct((cases, rows), F32),) * 4
        + (jax.ShapeDtypeStruct((cases, LANE), F32),),
        in_specs=[hbm, vmem, vmem, hbm, vmem, vmem],
        out_specs=(hbm,) * 4 + (vmem,),
        scratch_shapes=[
            pltpu.VMEM((subs, own, order), BF16),
            pltpu.VMEM((cases, rows + 2 * LANE), F32),
            pltpu.VMEM((cases, rows), F32),
            pltpu.VMEM((cases, rows), F32),
            pltpu.VMEM((cases, rows), F32),
            pltpu.VMEM((2, cases, rows), F32),
            pltpu.VMEM((cases, rows + 2 * LANE), BF16),
            pltpu.VMEM((2, cases, margin + LANE), BF16),
            pltpu.VMEM((steps, 2, cases, margin + LANE), BF16),
            pltpu.VMEM((2, cases, LANE), F32),
            pltpu.VMEM((2, cases, LANE), BF16),
            pltpu.VMEM((OUTER, 2, cases, LANE), BF16),
            pltpu.VMEM((LANE, rows + 2 * LANE), BF16),
            pltpu.VMEM((LANE, ns * LANE), BF16),
            pltpu.VMEM((LANE, ns * LANE), BF16),
            pltpu.VMEM((OUTER, cases, ns * LANE), BF16),
            pltpu.VMEM((2, cases, LANE), F32),
            pltpu.VMEM((OUTER, ns, 8, LANE), F32),
            dma, dma((4,)), dma((own // tile,)),
            dma((steps, 2)), dma((steps, 2)),
            dma((OUTER, 2)), dma((OUTER, 2)),
            dma((nl,)), dma((nl,)),
            dma((4,)), dma((4,)),
            dma((OUTER, ns)), dma((OUTER, ns)),
            dma((OUTER, ns)), dma((OUTER, ns)),
        ],
        compiler_params=pltpu.CompilerParams(
            collective_id=0, has_side_effects=True, vmem_limit_bytes=56 * 1024 * 1024
        ),
        cost_estimate=pl.CostEstimate(
            flops=flops, bytes_accessed=2 * subs * own * order, transcendentals=0
        ),
    )(right_side, diagonal[None, :], coupling[None, :], local_inverse, coarse_basis, coarse_inverse)
    group = 16
    wide = pl.BlockSpec((group, rows), lambda i: (i, 0))
    return pl.pallas_call(
        last_kernel,
        grid=(cases // group,),
        out_shape=(jax.ShapeDtypeStruct((cases, rows), F32),) * 2,
        in_specs=[pl.BlockSpec((group, LANE), lambda i: (i, 0))] + [wide] * 4,
        out_specs=(wide, wide),
        compiler_params=pltpu.CompilerParams(vmem_limit_bytes=16 * 1024 * 1024),
    )(alpha, solved, update, residual, image)


def solution(mesh):
    in_specs = (
        P("lift", "sector"),
        P("sector"),
        P("sector"),
        P("sector", None, None),
        P("sector", None, None),
        P("sector", "lift"),
    )
    out_specs = (P("lift", "sector"), P("lift", "sector"))
    return jax.shard_map(body, mesh=mesh, in_specs=in_specs, out_specs=out_specs, check_vma=False)
```

time: 116 us -> 103 us (0.89)
  Pallas kernels: 111 us -> 96.3 us
  local copies, waits for them, and re-layouts: 0.86 us -> 5.65 us
  other arithmetic: 3.82 us -> 0 us
    pallas_call x1, Pallas kernels: 111 us -> 94.3 us  [body(): pl.pallas_call(functools.partial(kernel, ns, nl), out_shape=(jax.ShapeDty...]
    unnamed x0 -> x10, local copies, waits for them, and re-layouts: none -> 5.65 us
    sub x1 -> x0, other arithmetic: 3.82 us -> none  [body(): return (solved + alpha * update, residual - alpha * image)]
    pallas_call x0 -> x1, Pallas kernels: none -> 1.96 us  [body(): pl.pallas_call(last_kernel, grid=(cases // group,), out_shape=(jax.ShapeD...]
where the time goes in v2:
time: 103 us
  Pallas kernels  96.3 us (93%)
  local copies, waits for them, and re-layouts  5.65 us (5%)
    pallas_call x1, Pallas kernels, body(): pl.pallas_call(functools.partial(kernel, ns, nl), out_shape=(jax.ShapeDty...  94.3 us
    unnamed x10, local copies, waits for them, and re-layouts  5.65 us

profile of v2, /device:TPU:0, one launch (start us, length us, event | category | flops | bytes accessed | tf_op | source)
XLA Modules:
  0.0 102.6 jit_solution(14680433503214758761)
XLA Ops:
  0.6 94.3 %shard_map.77 = (f32[64,4096]{1,0:T(8,128)}, f32[64,4096]{1,0:T(8,128)}, f32[64,4096]{1,0:T(8,128)}, f32[64,4096]{1,0:T(8,128)}, f32[64,128]{1,0:T(8,128)}) custom-call(f32[64,4096]{1,0:T(8,128)} %rhs_ref.1, f32[1,4096]{1,0:T(1,128)} %bitcast.2, f32[1,4096]{1,0:T(1,128)} %bitcast.3, bf16[4,1024,2048]{2,1,0:T(8,128)(2,1)} %inv_ref.1, ...), custom_call_target="tpu_custom_call" | custom-call | flops 8589934592 | bytes 16777216 | tf_op jit(solution)/shard_map/pallas_call | solution.py:477
  95.0 0.0 copy-start
  95.0 1.2 %copy-done = f32[64,4096]{1,0:T(8,128)S(1)} copy-done((f32[64,4096]{1,0:T(8,128)S(1)}, f32[64,4096]{1,0:T(8,128)}, u32[]{:S(2)}) %copy-start) | copy-done | bytes 1048600
  96.2 0.0 copy-start.1
  96.2 1.2 %copy-done.1 = f32[64,4096]{1,0:T(8,128)S(1)} copy-done((f32[64,4096]{1,0:T(8,128)S(1)}, f32[64,4096]{1,0:T(8,128)}, u32[]{:S(2)}) %copy-start.1) | copy-done | bytes 1048600
  97.4 0.0 copy-start.2
  97.4 1.2 %copy-done.2 = f32[64,4096]{1,0:T(8,128)S(1)} copy-done((f32[64,4096]{1,0:T(8,128)S(1)}, f32[64,4096]{1,0:T(8,128)}, u32[]{:S(2)}) %copy-start.2) | copy-done | bytes 1048600
  98.6 0.0 copy-start.3
  98.6 1.2 %copy-done.3 = f32[64,4096]{1,0:T(8,128)S(1)} copy-done((f32[64,4096]{1,0:T(8,128)S(1)}, f32[64,4096]{1,0:T(8,128)}, u32[]{:S(2)}) %copy-start.3) | copy-done | bytes 1048600
  99.9 0.0 copy-start.4
  99.9 0.8 copy-done.4
  100.6 2.0 %shard_map.78 = (f32[64,4096]{1,0:T(8,128)}, f32[64,4096]{1,0:T(8,128)}) custom-call(f32[64,128]{1,0:T(8,128)S(1)} %copy-done.4, f32[64,4096]{1,0:T(8,128)S(1)} %copy-done, f32[64,4096]{1,0:T(8,128)S(1)} %copy-done.2, f32[64,4096]{1,0:T(8,128)S(1)} %copy-done.1, f32[64,4096]{1,0:T(8,128)S(1)} %copy-done.3), custom_call_target="tpu_custom_call" | custom-call | tf_op jit(solution)/shard_map/pallas_call | solution.py:519
Async XLA Ops:
  95.0 1.2 %copy-start = (f32[64,4096]{1,0:T(8,128)S(1)}, f32[64,4096]{1,0:T(8,128)}, u32[]{:S(2)}) copy-start(f32[64,4096]{1,0:T(8,128)} %get-tuple-element.8.sol_ref) | copy-start | bytes 3145732
  96.2 1.2 %copy-start.1 = (f32[64,4096]{1,0:T(8,128)S(1)}, f32[64,4096]{1,0:T(8,128)}, u32[]{:S(2)}) copy-start(f32[64,4096]{1,0:T(8,128)} %get-tuple-element.10.res_ref) | copy-start | bytes 3145732
  97.4 1.2 %copy-start.2 = (f32[64,4096]{1,0:T(8,128)S(1)}, f32[64,4096]{1,0:T(8,128)}, u32[]{:S(2)}) copy-start(f32[64,4096]{1,0:T(8,128)} %get-tuple-element.9.last_ref) | copy-start | bytes 3145732
  98.6 1.2 %copy-start.3 = (f32[64,4096]{1,0:T(8,128)S(1)}, f32[64,4096]{1,0:T(8,128)}, u32[]{:S(2)}) copy-start(f32[64,4096]{1,0:T(8,128)} %get-tuple-element.11.img_ref) | copy-start | bytes 3145732
  99.9 0.8 copy-start.4

commit v3 on v2

--- a/solution.py
+++ b/solution.py
@@ -27,9 +27,9 @@
     ns, nl,
     rhs_ref, diag_ref, coup_ref, inv_ref, basis_ref, cinv_ref,
     sol_out, res_out, last_out, img_out, alpha_ref,
-    wv, u, keep, first, sol, field, h, snd, rcv, edge, esnd, ercv, bext, cx, cy, gbuf, stat, sbuf,
+    wv, u, sol, field, h, far, snd, rcv, edge, esnd, ercv, bext, cx, cy, gbuf, stat, sbuf,
     r_sem, o_sem, w_sem, hs_sem, hr_sem, es_sem, er_sem, ls_sem, lr_sem, ns_sem, nr_sem,
-    gs_sem, gr_sem, ss_sem, sr_sem,
+    gs_sem, gr_sem, fs_sem, fr_sem, ss_sem, sr_sem, bs_sem, br_sem,
 ):
     cases, rows = rhs_ref.shape
     subs, own, order = inv_ref.shape
@@ -164,17 +164,34 @@
             remote(esnd.at[1], ercv.at[o, 1], es_sem.at[o, 1], er_sem.at[o, 1], {"sector": left}),
         )
 
-    def gather_copy(o, k):
-        return remote(
-            gbuf.at[o, :, pl.ds(pl.multiple_of(me * LANE, LANE), LANE)],
-            gbuf.at[o, :, pl.ds(pl.multiple_of(me * LANE, LANE), LANE)],
-            gs_sem.at[o, k], gr_sem.at[o, k], {"sector": lax.rem(me + k, ns)},
-        )
-
-    def gather_wait(o, k):
-        source = lax.rem(me + ns - k, ns)
-        part = gbuf.at[o, :, pl.ds(pl.multiple_of(source * LANE, LANE), LANE)]
-        return remote(part, part, gs_sem.at[o, k], gr_sem.at[o, k], {"sector": lax.rem(me + k, ns)})
+    core = lax.rem(me, 2)
+    chip = me // 2
+    chips = ns // 2
+    sibling = me + 1 - 2 * core
+
+    def block_of(o, source):
+        return gbuf.at[o, :, pl.ds(pl.multiple_of(source * LANE, LANE), LANE)]
+
+    def gather_copy(o, k, source):
+        target = sibling if isinstance(k, int) else 2 * lax.rem(chip + k, chips) + core
+        part = block_of(o, source)
+        return remote(part, part, gs_sem.at[o, k], gr_sem.at[o, k], {"sector": target})
+
+    def hand_on(o, k, core_at):
+        part = block_of(o, 2 * lax.rem(chip + chips - k, chips) + core_at)
+        return remote(part, part, fs_sem.at[o, k], fr_sem.at[o, k], {"sector": sibling})
+
+    def far_copies(at, which):
+        return (
+            remote(
+                field.at[which, :, rows - margin:rows], far.at[at, 0],
+                bs_sem.at[at, 0], br_sem.at[at, 0], {"sector": right},
+            ),
+            remote(
+                field.at[which, :, 0:margin], far.at[at, 1],
+                bs_sem.at[at, 1], br_sem.at[at, 1], {"sector": left},
+            ),
+        )
 
     def sum_copy(o, k):
         return remote(
@@ -189,10 +206,10 @@
             {"sector": lax.rem(me + k, ns)},
         )
 
-    def sweep(t, src):
+    def residual_step(t):
         def low_rows(g, carry):
             rs = pl.ds(pl.multiple_of(g * group, group), group)
-            hf = field[src, rs, 0:margin] - applied(rs, 0, margin)
+            hf = field[0, rs, 0:margin] - applied(rs, 0, margin)
             hb = hf.astype(BF16)
             h[rs, LANE:LANE + margin] = hb
             snd[1, rs, 0:margin] = hb
@@ -200,7 +217,7 @@
             snd[1, rs, margin:margin + LANE] = pack(
                 [u[rs, LANE:LANE + 1], hf[:, 0:1], jnp.broadcast_to(coup_ref[:, 0:1], (group, 1))]
             )
-            hf = field[src, rs, rows - margin:rows] - applied(rs, rows - margin, margin)
+            hf = field[0, rs, rows - margin:rows] - applied(rs, rows - margin, margin)
             hb = hf.astype(BF16)
             h[rs, LANE + rows - margin:LANE + rows] = hb
             snd[0, rs, 0:margin] = hb
@@ -222,21 +239,13 @@
             rs = pl.ds(pl.multiple_of(g * group, group), group)
             for at in range(margin, rows - margin, own):
                 width = min(own, rows - margin - at)
-                hf = field[src, rs, at:at + width] - applied(rs, at, width)
+                hf = field[0, rs, at:at + width] - applied(rs, at, width)
                 h[rs, LANE + at:LANE + at + width] = hf.astype(BF16)
             return carry
 
         lax.fori_loop(0, groups, middle_rows, 0)
 
-        @pl.when(t == 0)
-        def _():
-            for k in range(1, nl):
-                lift_wait(k).wait()
-            for copy in neighbour_copies():
-                copy.start()
-            for i in range(tiles):
-                w_copy(i).wait()
-
+    def inner_products():
         def inner(i, carry):
             ws = pl.ds(pl.multiple_of(i * tile, tile), tile)
             for j in range(subs):
@@ -248,7 +257,9 @@
             return carry
 
         lax.fori_loop(0, tiles, inner, 0, unroll=True)
-        for copy in copies:
+
+    def take_halos(t):
+        for copy in halo_copies(t):
             copy.wait()
         msg_low = rcv[t, 0, :, margin:margin + LANE].astype(F32)
         msg_high = rcv[t, 1, :, margin:margin + LANE].astype(F32)
@@ -271,6 +282,7 @@
             lane_c == 0, part(msg_high, 1) + part(msg_high, 2) * part(mine_high, 0), halo_high
         ).astype(BF16)
 
+    def outer_products(t):
         def outer_part(i, carry):
             ws = pl.ds(pl.multiple_of(i * tile, tile), tile)
             out = pl.ds(pl.multiple_of(LANE + i * tile, LANE), tile)
@@ -335,10 +347,11 @@
         gbuf[o, :, pl.ds(pl.multiple_of(me * LANE, LANE), LANE)] = projected.astype(BF16)
 
         def start_gather(k, carry):
-            gather_copy(o, k).start()
-            return carry
-
-        lax.fori_loop(1, ns, start_gather, 0)
+            gather_copy(o, k, me).start()
+            return carry
+
+        lax.fori_loop(1, chips, start_gather, 0)
+        gather_copy(o, 0, me).start()
         for copy in rims:
             copy.wait()
         msg = ercv[o, 0].astype(F32)
@@ -346,11 +359,22 @@
         msg = ercv[o, 1].astype(F32)
         u[:, LANE + rows:2 * LANE + rows] = jnp.broadcast_to(part(msg, 0), (cases, LANE))
 
+        def pass_on(k, carry):
+            gather_copy(o, k, 2 * lax.rem(chip + chips - k, chips) + core).wait_recv()
+            hand_on(o, k, core).start()
+            return carry
+
+        lax.fori_loop(1, chips, pass_on, 0)
+
         def wait_gather(k, carry):
-            gather_wait(o, k).wait()
-            return carry
-
-        lax.fori_loop(1, ns, wait_gather, 0)
+            gather_copy(o, k, me).wait_send()
+            hand_on(o, k, core).wait_send()
+            hand_on(o, k, 1 - core).wait_recv()
+            return carry
+
+        gather_copy(o, 0, me).wait_send()
+        gather_copy(o, 0, sibling).wait_recv()
+        lax.fori_loop(1, chips, wait_gather, 0)
         coarse = dot_nt(gbuf[o], cy[...]).astype(BF16)
         step = 2 * LANE
         for at in range(0, 2 * LANE + rows, step):
@@ -374,18 +398,22 @@
             return carry
 
         lax.fori_loop(0, groups, image_rows, 0)
-        line = lax.broadcasted_iota(jnp.int32, (8, LANE), 0)
         row_sums = [
             jnp.sum(jnp.where(eye, jnp.sum(stat[at], axis=1, keepdims=True), 0.0), axis=0, keepdims=True)
             for at in range(2)
         ]
-        sbuf[o, me] = jnp.where(line == 0, row_sums[0], jnp.where(line == 1, row_sums[1], 0.0))
+        sbuf[o, me] = row_sums[0] + pltpu.roll(row_sums[1], LANE // 2, 1)
 
         def start_sum(k, carry):
             sum_copy(o, k).start()
             return carry
 
         lax.fori_loop(1, ns, start_sum, 0)
+
+        @pl.when(o < OUTER - 1)
+        def _():
+            for copy in far_copies(o + 1, 1):
+                copy.start()
 
     def get_alpha(o):
         def wait_sum(k, carry):
@@ -394,7 +422,7 @@
 
         lax.fori_loop(1, ns, wait_sum, 0)
         totals = jnp.sum(sbuf[o], axis=0)
-        alpha_row = totals[0:1] / (totals[1:2] + 1e-06)
+        alpha_row = totals / (pltpu.roll(totals, LANE // 2, 1) + 1e-06)
         alpha_ref[...] = jnp.broadcast_to(
             jnp.sum(jnp.where(eye, alpha_row, 0.0), axis=1, keepdims=True), (cases, LANE)
         )
@@ -405,45 +433,74 @@
         for c in range(subs):
             cols = slice(c * own, (c + 1) * own)
             wide = slice(LANE + c * own, LANE + (c + 1) * own)
-            sol[rs, cols] += alpha * keep[rs, cols]
-            field[0, rs, cols] -= alpha * field[1, rs, cols]
-            begun = first[rs, cols] - alpha * u[rs, wide]
-            u[rs, wide] = begun
-            if OUTER > 2:
-                first[rs, cols] = begun
+            sol[rs, cols] += alpha * u[rs, wide]
+            u[rs, wide] = jnp.zeros((group, own), F32)
+            fresh = field[0, rs, cols] - alpha * field[1, rs, cols]
+            field[0, rs, cols] = fresh
+            h[rs, wide] = fresh.astype(BF16)
         return carry
 
     rhs_copy.wait()
+    for copy in far_copies(0, 0):
+        copy.start()
+    h[:, LANE:LANE + rows] = field[0].astype(BF16)
+    for k in range(1, nl):
+        lift_wait(k).wait()
+    for copy in neighbour_copies():
+        copy.start()
+    for i in range(tiles):
+        w_copy(i).wait()
 
     def turn(t, carry):
         o = t // SWEEPS
         begins = lax.rem(t, SWEEPS) == 0
-        later = jnp.logical_and(begins, t > 0)
-        sweep(t, jnp.where(later, 1, 0))
-
-        @pl.when(t == 0)
-        def _():
-            first[...] = u[:, LANE:LANE + rows]
-            complete_coarse()
-
-        @pl.when(later)
+
+        @pl.when(jnp.logical_and(begins, t > 0))
         def _():
             get_alpha(o - 1)
             lax.fori_loop(0, groups, next_rows, 0)
+            u[:, 0:LANE] = jnp.zeros((cases, LANE), F32)
+            u[:, LANE + rows:2 * LANE + rows] = jnp.zeros((cases, LANE), F32)
+            for copy in far_copies(o, 1):
+                copy.wait()
+            alpha = alpha_ref[:, 0:1]
+            for side in range(2):
+                far[0, side] = far[0, side] - alpha * far[o, side]
 
         @pl.when(t == (OUTER - 1) * SWEEPS)
         def _():
             for copy in result_copies[:2]:
                 copy.start()
 
+        @pl.when(jnp.logical_not(begins))
+        def _():
+            residual_step(t)
+
+        inner_products()
+
+        @pl.when(t == 0)
+        def _():
+            for copy in far_copies(0, 0):
+                copy.wait()
+
+        @pl.when(begins)
+        def _():
+            for side in range(2):
+                rcv[t, side, :, 0:margin] = far[0, side].astype(BF16)
+
+        @pl.when(jnp.logical_not(begins))
+        def _():
+            take_halos(t)
+
+        outer_products(t)
+
+        @pl.when(t == 0)
+        def _():
+            complete_coarse()
+
         @pl.when(lax.rem(t, SWEEPS) == SWEEPS - 1)
         def _():
             coarse_step(t, o)
-
-            @pl.when(o < OUTER - 1)
-            def _():
-                keep[...] = u[:, LANE:LANE + rows]
-                u[...] = jnp.zeros_like(u)
 
         return carry
 
@@ -484,10 +541,9 @@
             pltpu.VMEM((subs, own, order), BF16),
             pltpu.VMEM((cases, rows + 2 * LANE), F32),
             pltpu.VMEM((cases, rows), F32),
-            pltpu.VMEM((cases, rows), F32),
-            pltpu.VMEM((cases, rows), F32),
             pltpu.VMEM((2, cases, rows), F32),
             pltpu.VMEM((cases, rows + 2 * LANE), BF16),
+            pltpu.VMEM((OUTER, 2, cases, margin), F32),
             pltpu.VMEM((2, cases, margin + LANE), BF16),
             pltpu.VMEM((steps, 2, cases, margin + LANE), BF16),
             pltpu.VMEM((2, cases, LANE), F32),
@@ -498,14 +554,16 @@
             pltpu.VMEM((LANE, ns * LANE), BF16),
             pltpu.VMEM((OUTER, cases, ns * LANE), BF16),
             pltpu.VMEM((2, cases, LANE), F32),
-            pltpu.VMEM((OUTER, ns, 8, LANE), F32),
+            pltpu.VMEM((OUTER, ns, 1, LANE), F32),
             dma, dma((4,)), dma((own // tile,)),
             dma((steps, 2)), dma((steps, 2)),
             dma((OUTER, 2)), dma((OUTER, 2)),
             dma((nl,)), dma((nl,)),
             dma((4,)), dma((4,)),
+            dma((OUTER, ns // 2)), dma((OUTER, ns // 2)),
+            dma((OUTER, ns // 2)), dma((OUTER, ns // 2)),
             dma((OUTER, ns)), dma((OUTER, ns)),
-            dma((OUTER, ns)), dma((OUTER, ns)),
+            dma((OUTER, 2)), dma((OUTER, 2)),
         ],
         compiler_params=pltpu.CompilerParams(
             collective_id=0, has_side_effects=True, vmem_limit_bytes=56 * 1024 * 1024
@@ -522,7 +580,7 @@
         out_shape=(jax.ShapeDtypeStruct((cases, rows), F32),) * 2,
         in_specs=[pl.BlockSpec((group, LANE), lambda i: (i, 0))] + [wide] * 4,
         out_specs=(wide, wide),
-        compiler_params=pltpu.CompilerParams(vmem_limit_bytes=16 * 1024 * 1024),
+        compiler_params=pltpu.CompilerParams(vmem_limit_bytes=56 * 1024 * 1024),
     )(alpha, solved, update, residual, image)
 
 

time: 103 us -> 98.8 us (0.959)
  local copies, waits for them, and re-layouts: 5.65 us -> 0 us
  Pallas kernels: 96.3 us -> 98 us
    unnamed x10 -> x0, local copies, waits for them, and re-layouts: 5.65 us -> none
    pallas_call x1, Pallas kernels: 1.96 us -> 4.29 us  [body(): pl.pallas_call(last_kernel, grid=(cases // group,), out_shape=(jax.ShapeD...]
where the time goes in v3:
time: 98.8 us; the launch traced here: 98.6 us
  Pallas kernels  98 us (99%)
    pallas_call x1, Pallas kernels, body(): pl.pallas_call(functools.partial(kernel, ns, nl), out_shape=(jax.ShapeDty...  93.7 us
    pallas_call x1, Pallas kernels, body(): pl.pallas_call(last_kernel, grid=(cases // group,), out_shape=(jax.ShapeD...  4.29 us

profile of v3, /device:TPU:0, one launch (start us, length us, event | category | flops | bytes accessed | tf_op | source)
XLA Modules:
  0.0 98.6 jit_solution(7923390190947672645)
XLA Ops:
  0.6 93.7 %shard_map.77 = (f32[64,4096]{1,0:T(8,128)}, f32[64,4096]{1,0:T(8,128)}, f32[64,4096]{1,0:T(8,128)}, f32[64,4096]{1,0:T(8,128)}, f32[64,128]{1,0:T(8,128)}) custom-call(f32[64,4096]{1,0:T(8,128)} %rhs_ref.1, f32[1,4096]{1,0:T(1,128)} %bitcast.2, f32[1,4096]{1,0:T(1,128)} %bitcast.3, bf16[4,1024,2048]{2,1,0:T(8,128)(2,1)} %inv_ref.1, ...), custom_call_target="tpu_custom_call" | custom-call | flops 8589934592 | bytes 16777216 | tf_op jit(solution)/shard_map/pallas_call | solution.py:534
  94.3 4.3 %shard_map.78 = (f32[64,4096]{1,0:T(8,128)}, f32[64,4096]{1,0:T(8,128)}) custom-call(f32[64,128]{1,0:T(8,128)} %get-tuple-element.7.alpha_ref, f32[64,4096]{1,0:T(8,128)} %get-tuple-element.8.sol_ref, f32[64,4096]{1,0:T(8,128)} %get-tuple-element.9.last_ref, f32[64,4096]{1,0:T(8,128)} %get-tuple-element.10.res_ref, f32[64,4096]{1,0:T(8,128)} %get-tuple-element.11.img_ref), custom_call_target="tpu_custom_call" | custom-call | tf_op jit(solution)/shard_map/pallas_call | solution.py:577

commit v4 on v3

--- a/solution.py
+++ b/solution.py
@@ -36,8 +36,8 @@
     margin = (order - own) // 2
     modes = basis_ref.shape[1]
     nm = subs * modes
-    tile = wv.shape[1] // w_sem.shape[0]
-    tiles = own // tile
+    tiles = w_sem.shape[1]
+    tile = own // tiles
     group = 16
     groups = cases // group
     cut = margin + 2 * LANE
@@ -46,15 +46,15 @@
     right = lax.rem(me + 1, ns)
     left = lax.rem(me + ns - 1, ns)
 
-    def w_copy(i):
-        return pltpu.make_async_copy(
-            inv_ref.at[:, pl.ds(i * tile, tile), :], wv.at[:, pl.ds(i * tile, tile), :], w_sem.at[i]
-        )
+    def w_copy(j, i):
+        some = pl.ds(i * tile, tile)
+        return pltpu.make_async_copy(inv_ref.at[j, some, :], wv.at[j, some, :], w_sem.at[j, i])
 
     rhs_copy = pltpu.make_async_copy(rhs_ref, field.at[0], r_sem)
     rhs_copy.start()
     for i in range(tiles):
-        w_copy(i).start()
+        for j in range(subs):
+            w_copy(j, i).start()
     result_copies = (
         pltpu.make_async_copy(sol, sol_out, o_sem.at[0]),
         pltpu.make_async_copy(field.at[0], res_out, o_sem.at[1]),
@@ -245,18 +245,21 @@
 
         lax.fori_loop(0, groups, middle_rows, 0)
 
-    def inner_products():
+    def inner_products(arriving=False):
         def inner(i, carry):
-            ws = pl.ds(pl.multiple_of(i * tile, tile), tile)
+            ws = pl.ds(i * tile, tile)
             for j in range(subs):
+                if arriving:
+                    w_copy(j, i).wait()
                 low = cut if j == 0 else 0
                 high = order - cut if j == subs - 1 else order
                 shift = LANE + j * own - margin
-                out = pl.ds(pl.multiple_of(LANE + j * own + i * tile, LANE), tile)
+                out = pl.ds(LANE + j * own + i * tile, tile)
                 u[:, out] += times(h[:, shift + low:shift + high], wv[j, ws, low:high]).T
             return carry
 
-        lax.fori_loop(0, tiles, inner, 0, unroll=True)
+        for i in range(tiles):
+            inner(i, 0)
 
     def take_halos(t):
         for copy in halo_copies(t):
@@ -448,14 +451,23 @@
         lift_wait(k).wait()
     for copy in neighbour_copies():
         copy.start()
-    for i in range(tiles):
-        w_copy(i).wait()
+    complete_coarse()
+    inner_products(arriving=True)
+    for copy in far_copies(0, 0):
+        copy.wait()
+
+    def known_halos(t):
+        for side in range(2):
+            rcv[t, side, :, 0:margin] = far[0, side].astype(BF16)
+
+    known_halos(0)
+    outer_products(0)
 
     def turn(t, carry):
         o = t // SWEEPS
         begins = lax.rem(t, SWEEPS) == 0
 
-        @pl.when(jnp.logical_and(begins, t > 0))
+        @pl.when(begins)
         def _():
             get_alpha(o - 1)
             lax.fori_loop(0, groups, next_rows, 0)
@@ -478,15 +490,9 @@
 
         inner_products()
 
-        @pl.when(t == 0)
-        def _():
-            for copy in far_copies(0, 0):
-                copy.wait()
-
         @pl.when(begins)
         def _():
-            for side in range(2):
-                rcv[t, side, :, 0:margin] = far[0, side].astype(BF16)
+            known_halos(t)
 
         @pl.when(jnp.logical_not(begins))
         def _():
@@ -494,17 +500,13 @@
 
         outer_products(t)
 
-        @pl.when(t == 0)
-        def _():
-            complete_coarse()
-
         @pl.when(lax.rem(t, SWEEPS) == SWEEPS - 1)
         def _():
             coarse_step(t, o)
 
         return carry
 
-    lax.fori_loop(0, OUTER * SWEEPS, turn, 0, unroll=False)
+    lax.fori_loop(1, OUTER * SWEEPS, turn, 0, unroll=False)
     for copy in result_copies[2:]:
         copy.start()
     get_alpha(OUTER - 1)
@@ -555,7 +557,7 @@
             pltpu.VMEM((OUTER, cases, ns * LANE), BF16),
             pltpu.VMEM((2, cases, LANE), F32),
             pltpu.VMEM((OUTER, ns, 1, LANE), F32),
-            dma, dma((4,)), dma((own // tile,)),
+            dma, dma((4,)), dma((subs, own // tile)),
             dma((steps, 2)), dma((steps, 2)),
             dma((OUTER, 2)), dma((OUTER, 2)),
             dma((nl,)), dma((nl,)),
@@ -566,7 +568,7 @@
             dma((OUTER, 2)), dma((OUTER, 2)),
         ],
         compiler_params=pltpu.CompilerParams(
-            collective_id=0, has_side_effects=True, vmem_limit_bytes=56 * 1024 * 1024
+            collective_id=0, has_side_effects=True, vmem_limit_bytes=46 * 1024 * 1024
         ),
         cost_estimate=pl.CostEstimate(
             flops=flops, bytes_accessed=2 * subs * own * order, transcendentals=0
@@ -580,7 +582,7 @@
         out_shape=(jax.ShapeDtypeStruct((cases, rows), F32),) * 2,
         in_specs=[pl.BlockSpec((group, LANE), lambda i: (i, 0))] + [wide] * 4,
         out_specs=(wide, wide),
-        compiler_params=pltpu.CompilerParams(vmem_limit_bytes=56 * 1024 * 1024),
+        compiler_params=pltpu.CompilerParams(vmem_limit_bytes=16 * 1024 * 1024),
     )(alpha, solved, update, residual, image)
 
 

time: 98.8 us -> 110 us (1.11)
  Pallas kernels: 98 us -> 104 us
  local copies, waits for them, and re-layouts: 0 us -> 4.46 us
    pallas_call x1, Pallas kernels: 93.7 us -> 102 us  [body(): pl.pallas_call(functools.partial(kernel, ns, nl), out_shape=(jax.ShapeDty...]
    unnamed x0 -> x10, local copies, waits for them, and re-layouts: none -> 4.46 us
    pallas_call x1, Pallas kernels: 4.29 us -> 1.99 us  [body(): pl.pallas_call(last_kernel, grid=(cases // group,), out_shape=(jax.ShapeD...]
where the time goes in v4:
time: 110 us; the launch traced here: 109 us
  Pallas kernels  104 us (95%)
  local copies, waits for them, and re-layouts  4.46 us (4%)
    pallas_call x1, Pallas kernels, body(): pl.pallas_call(functools.partial(kernel, ns, nl), out_shape=(jax.ShapeDty...  102 us
    unnamed x10, local copies, waits for them, and re-layouts  4.46 us

profile of v4, /device:TPU:0, one launch (start us, length us, event | category | flops | bytes accessed | tf_op | source)
XLA Modules:
  0.0 109.4 jit_solution(11190700802112649284)
XLA Ops:
  0.6 0.0 copy-start
  0.6 1.2 %copy-done = f32[64,4096]{1,0:T(8,128)S(1)} copy-done((f32[64,4096]{1,0:T(8,128)S(1)}, f32[64,4096]{1,0:T(8,128)}, u32[]{:S(2)}) %copy-start) | copy-done | bytes 1048600
  1.9 0.0 copy-start.1
  1.9 0.9 copy-done.1
  2.8 0.0 copy-start.2
  2.8 0.9 copy-done.2
  3.7 0.0 copy-start.3
  3.7 0.7 copy-done.3
  4.4 0.0 copy-start.4
  4.4 0.7 copy-done.4
  5.1 102.3 %shard_map.77 = (f32[64,4096]{1,0:T(8,128)S(1)}, f32[64,4096]{1,0:T(8,128)S(1)}, f32[64,4096]{1,0:T(8,128)S(1)}, f32[64,4096]{1,0:T(8,128)S(1)}, f32[64,128]{1,0:T(8,128)S(1)}) custom-call(f32[64,4096]{1,0:T(8,128)S(1)} %copy-done, f32[1,4096]{1,0:T(1,128)S(1)} %bitcast.2, f32[1,4096]{1,0:T(1,128)S(1)} %bitcast.3, bf16[4,1024,2048]{2,1,0:T(8,128)(2,1)} %inv_ref.1, ...), custom_call_target="tpu_custom_call" | custom-call | flops 8589934592 | bytes 16777216 | tf_op jit(solution)/shard_map/pallas_call | solution.py:536
  107.4 2.0 %shard_map.78 = (f32[64,4096]{1,0:T(8,128)}, f32[64,4096]{1,0:T(8,128)}) custom-call(f32[64,128]{1,0:T(8,128)S(1)} %get-tuple-element.7.alpha_ref, f32[64,4096]{1,0:T(8,128)S(1)} %get-tuple-element.8.sol_ref, f32[64,4096]{1,0:T(8,128)S(1)} %get-tuple-element.9.last_ref, f32[64,4096]{1,0:T(8,128)S(1)} %get-tuple-element.10.res_ref, ...), custom_call_target="tpu_custom_call" | custom-call | tf_op jit(solution)/shard_map/pallas_call | solution.py:579
Async XLA Ops:
  0.6 1.2 %copy-start = (f32[64,4096]{1,0:T(8,128)S(1)}, f32[64,4096]{1,0:T(8,128)}, u32[]{:S(2)}) copy-start(f32[64,4096]{1,0:T(8,128)} %rhs_ref.1) | copy-start | bytes 3145732
  1.9 0.9 copy-start.1
  2.8 0.9 copy-start.2
  3.7 0.7 copy-start.3
  4.4 0.7 copy-start.4

commit v5 on v3

--- a/solution.py
+++ b/solution.py
@@ -27,7 +27,7 @@
     ns, nl,
     rhs_ref, diag_ref, coup_ref, inv_ref, basis_ref, cinv_ref,
     sol_out, res_out, last_out, img_out, alpha_ref,
-    wv, u, sol, field, h, far, snd, rcv, edge, esnd, ercv, bext, cx, cy, gbuf, stat, sbuf,
+    wv, u, sol, field, h, hold, far, snd, rcv, edge, esnd, ercv, bext, cx, cy, gbuf, stat, sbuf,
     r_sem, o_sem, w_sem, hs_sem, hr_sem, es_sem, er_sem, ls_sem, lr_sem, ns_sem, nr_sem,
     gs_sem, gr_sem, fs_sem, fr_sem, ss_sem, sr_sem, bs_sem, br_sem,
 ):
@@ -69,9 +69,24 @@
         )
 
     bext[...] = jnp.zeros_like(bext)
+    cx[...] = jnp.zeros_like(cx)
+    barrier = pltpu.get_barrier_semaphore()
+
+    def greet(k, carry):
+        pl.semaphore_signal(
+            barrier, inc=1, device_id={"sector": lax.rem(me + k, ns)},
+            device_id_type=pl.DeviceIdType.MESH,
+        )
+        return carry
+
+    lax.fori_loop(1, ns, greet, 0)
+    for k in range(1, nl):
+        pl.semaphore_signal(
+            barrier, inc=1, device_id={"lift": lax.rem(lift + k, nl)},
+            device_id_type=pl.DeviceIdType.MESH,
+        )
     for j in range(subs):
         bext[j * modes:(j + 1) * modes, LANE + j * own:LANE + (j + 1) * own] = basis_ref[j]
-    cx[...] = jnp.zeros_like(cx)
     half = cinv_ref.shape[1]
     per = half // nm
     lanes = lax.broadcasted_iota(jnp.int32, (nm, LANE), 1)
@@ -83,21 +98,6 @@
             block = pltpu.roll(block, LANE - (start - base), 1)
         block = jnp.where(lanes < nm, block, 0.0).astype(BF16)
         cx[0:nm, pl.ds(pl.multiple_of((lift * per + d) * LANE, LANE), LANE)] = block
-    barrier = pltpu.get_barrier_semaphore()
-
-    def greet(k, carry):
-        pl.semaphore_signal(
-            barrier, inc=1, device_id={"sector": lax.rem(me + k, ns)},
-            device_id_type=pl.DeviceIdType.MESH,
-        )
-        return carry
-
-    lax.fori_loop(1, ns, greet, 0)
-    for k in range(1, nl):
-        pl.semaphore_signal(
-            barrier, inc=1, device_id={"lift": lax.rem(lift + k, nl)},
-            device_id_type=pl.DeviceIdType.MESH,
-        )
     h[...] = jnp.zeros_like(h)
     u[...] = jnp.zeros_like(u)
     sol[...] = jnp.zeros_like(sol)
@@ -234,6 +234,7 @@
         copies = halo_copies(t)
         for copy in copies:
             copy.start()
+        outer_products(t - 1, False)
 
         def middle_rows(g, carry):
             rs = pl.ds(pl.multiple_of(g * group, group), group)
@@ -282,25 +283,27 @@
             lane_c == 0, part(msg_high, 1) + part(msg_high, 2) * part(mine_high, 0), halo_high
         ).astype(BF16)
 
-    def outer_products(t):
-        def outer_part(i, carry):
-            ws = pl.ds(pl.multiple_of(i * tile, tile), tile)
-            out = pl.ds(pl.multiple_of(LANE + i * tile, LANE), tile)
-            u[:, out] += (
-                times(rcv[t, 0, :, 0:margin], wv[0, ws, 0:margin])
-                + times(h[:, LANE:LANE + cut - margin], wv[0, ws, margin:cut])
-            ).T
-            out = pl.ds(pl.multiple_of(LANE + (subs - 1) * own + i * tile, LANE), tile)
-            u[:, out] += (
-                times(rcv[t, 1, :, 0:margin], wv[subs - 1, ws, order - margin:order])
-                + times(
-                    h[:, LANE + rows - (cut - margin):LANE + rows],
-                    wv[subs - 1, ws, order - cut:order - margin],
-                )
-            ).T
-            return carry
-
-        lax.fori_loop(0, tiles, outer_part, 0, unroll=True)
+    def keep_rims():
+        inside = cut - margin
+        hold[0] = h[:, LANE:LANE + inside]
+        hold[1] = h[:, LANE + rows - inside:LANE + rows]
+
+    def outer_products(t, near):
+        reach = margin + LANE
+        spans = (
+            ((0, reach), (own - reach, own)) if near else ((reach, own), (0, own - reach))
+        )
+        low, high = spans
+        last = subs - 1
+        u[:, LANE + low[0]:LANE + low[1]] += (
+            times(rcv[t, 0, :, 0:margin], wv[0, low[0]:low[1], 0:margin])
+            + times(hold[0], wv[0, low[0]:low[1], margin:cut])
+        ).T
+        base = LANE + last * own
+        u[:, base + high[0]:base + high[1]] += (
+            times(rcv[t, 1, :, 0:margin], wv[last, high[0]:high[1], order - margin:order])
+            + times(hold[1], wv[last, high[0]:high[1], order - cut:order - margin])
+        ).T
 
     def complete_coarse():
         for copy in neighbour_copies():
@@ -444,10 +447,6 @@
     for copy in far_copies(0, 0):
         copy.start()
     h[:, LANE:LANE + rows] = field[0].astype(BF16)
-    for k in range(1, nl):
-        lift_wait(k).wait()
-    for copy in neighbour_copies():
-        copy.start()
     for i in range(tiles):
         w_copy(i).wait()
 
@@ -480,9 +479,17 @@
 
         @pl.when(t == 0)
         def _():
+            for k in range(1, nl):
+                lift_wait(k).wait()
+            for copy in neighbour_copies():
+                copy.start()
             for copy in far_copies(0, 0):
                 copy.wait()
 
+        @pl.when(t == 1)
+        def _():
+            complete_coarse()
+
         @pl.when(begins)
         def _():
             for side in range(2):
@@ -492,14 +499,12 @@
         def _():
             take_halos(t)
 
-        outer_products(t)
-
-        @pl.when(t == 0)
-        def _():
-            complete_coarse()
+        keep_rims()
+        outer_products(t, True)
 
         @pl.when(lax.rem(t, SWEEPS) == SWEEPS - 1)
         def _():
+            outer_products(t, False)
             coarse_step(t, o)
 
         return carry
@@ -543,6 +548,7 @@
             pltpu.VMEM((cases, rows), F32),
             pltpu.VMEM((2, cases, rows), F32),
             pltpu.VMEM((cases, rows + 2 * LANE), BF16),
+            pltpu.VMEM((2, cases, 2 * LANE), BF16),
             pltpu.VMEM((OUTER, 2, cases, margin), F32),
             pltpu.VMEM((2, cases, margin + LANE), BF16),
             pltpu.VMEM((steps, 2, cases, margin + LANE), BF16),
@@ -572,7 +578,7 @@
             flops=flops, bytes_accessed=2 * subs * own * order, transcendentals=0
         ),
     )(right_side, diagonal[None, :], coupling[None, :], local_inverse, coarse_basis, coarse_inverse)
-    group = 16
+    group = 8
     wide = pl.BlockSpec((group, rows), lambda i: (i, 0))
     return pl.pallas_call(
         last_kernel,

time: 98.8 us -> 98.9 us (level)
    pallas_call x1, Pallas kernels: 93.7 us -> 91.6 us  [body(): pl.pallas_call(functools.partial(kernel, ns, nl), out_shape=(jax.ShapeDty...]
    pallas_call x1, Pallas kernels: 4.29 us -> 6.38 us  [body(): pl.pallas_call(last_kernel, grid=(cases // group,), out_shape=(jax.ShapeD...]
where the time goes in v5:
time: 98.9 us; the launch traced here: 98.6 us
  Pallas kernels  98 us (99%)
    pallas_call x1, Pallas kernels, body(): pl.pallas_call(functools.partial(kernel, ns, nl), out_shape=(jax.ShapeDty...  91.6 us
    pallas_call x1, Pallas kernels, body(): pl.pallas_call(last_kernel, grid=(cases // group,), out_shape=(jax.ShapeD...  6.38 us

profile of v5, /device:TPU:0, one launch (start us, length us, event | category | flops | bytes accessed | tf_op | source)
XLA Modules:
  0.0 98.6 jit_solution(10772280083645161666)
XLA Ops:
  0.6 91.6 %shard_map.77 = (f32[64,4096]{1,0:T(8,128)}, f32[64,4096]{1,0:T(8,128)}, f32[64,4096]{1,0:T(8,128)}, f32[64,4096]{1,0:T(8,128)}, f32[64,128]{1,0:T(8,128)}) custom-call(f32[64,4096]{1,0:T(8,128)} %rhs_ref.1, f32[1,4096]{1,0:T(1,128)} %bitcast.2, f32[1,4096]{1,0:T(1,128)} %bitcast.3, bf16[4,1024,2048]{2,1,0:T(8,128)(2,1)} %inv_ref.1, ...), custom_call_target="tpu_custom_call" | custom-call | flops 8589934592 | bytes 16777216 | tf_op jit(solution)/shard_map/pallas_call | solution.py:539
  92.2 6.4 %shard_map.78 = (f32[64,4096]{1,0:T(8,128)}, f32[64,4096]{1,0:T(8,128)}) custom-call(f32[64,128]{1,0:T(8,128)} %get-tuple-element.7.alpha_ref, f32[64,4096]{1,0:T(8,128)} %get-tuple-element.8.sol_ref, f32[64,4096]{1,0:T(8,128)} %get-tuple-element.9.last_ref, f32[64,4096]{1,0:T(8,128)} %get-tuple-element.10.res_ref, f32[64,4096]{1,0:T(8,128)} %get-tuple-element.11.img_ref), custom_call_target="tpu_custom_call" | custom-call | tf_op jit(solution)/shard_map/pallas_call | solution.py:583

commit v6 on v5

--- a/solution.py
+++ b/solution.py
@@ -578,7 +578,7 @@
             flops=flops, bytes_accessed=2 * subs * own * order, transcendentals=0
         ),
     )(right_side, diagonal[None, :], coupling[None, :], local_inverse, coarse_basis, coarse_inverse)
-    group = 8
+    group = 32
     wide = pl.BlockSpec((group, rows), lambda i: (i, 0))
     return pl.pallas_call(
         last_kernel,

time: 98.9 us -> 95.7 us (0.968)
  Pallas kernels: 98 us -> 94.9 us
    pallas_call x1, Pallas kernels: 6.38 us -> 3.32 us  [body(): pl.pallas_call(last_kernel, grid=(cases // group,), out_shape=(jax.ShapeD...]
where the time goes in v6:
time: 95.7 us; the launch traced here: 95.5 us
  Pallas kernels  94.9 us (99%)
    pallas_call x1, Pallas kernels, body(): pl.pallas_call(functools.partial(kernel, ns, nl), out_shape=(jax.ShapeDty...  91.6 us
    pallas_call x1, Pallas kernels, body(): pl.pallas_call(last_kernel, grid=(cases // group,), out_shape=(jax.ShapeD...  3.32 us

profile of v6, /device:TPU:0, one launch (start us, length us, event | category | flops | bytes accessed | tf_op | source)
XLA Modules:
  0.0 95.5 jit_solution(11970787113447844753)
XLA Ops:
  0.6 91.6 %shard_map.77 = (f32[64,4096]{1,0:T(8,128)}, f32[64,4096]{1,0:T(8,128)}, f32[64,4096]{1,0:T(8,128)}, f32[64,4096]{1,0:T(8,128)}, f32[64,128]{1,0:T(8,128)}) custom-call(f32[64,4096]{1,0:T(8,128)} %rhs_ref.1, f32[1,4096]{1,0:T(1,128)} %bitcast.2, f32[1,4096]{1,0:T(1,128)} %bitcast.3, bf16[4,1024,2048]{2,1,0:T(8,128)(2,1)} %inv_ref.1, ...), custom_call_target="tpu_custom_call" | custom-call | flops 8589934592 | bytes 16777216 | tf_op jit(solution)/shard_map/pallas_call | solution.py:539
  92.2 3.3 %shard_map.78 = (f32[64,4096]{1,0:T(8,128)}, f32[64,4096]{1,0:T(8,128)}) custom-call(f32[64,128]{1,0:T(8,128)} %get-tuple-element.7.alpha_ref, f32[64,4096]{1,0:T(8,128)} %get-tuple-element.8.sol_ref, f32[64,4096]{1,0:T(8,128)} %get-tuple-element.9.last_ref, f32[64,4096]{1,0:T(8,128)} %get-tuple-element.10.res_ref, f32[64,4096]{1,0:T(8,128)} %get-tuple-element.11.img_ref), custom_call_target="tpu_custom_call" | custom-call | tf_op jit(solution)/shard_map/pallas_call | solution.py:583
